TPU v7x, 512 devices: a whole 4x8x8 slice. The times are simulated.
512 devices in a mesh: task: 16 (over y, core), tile: 32 (over x, z).
Axes of the slice: x: 4, y: 8, z: 8, core: 2. Of those that a mesh axis runs over, the one named last changes fastest.
Arguments:
- deltas: bfloat16 [16, 4096, 16384], P('task', None, 'tile'), may hold values from -8 to 8
- sketches: bfloat16 [16, 16384, 16], P('task', 'tile'), may hold values from -6 to 6
Outputs:
- merged: bfloat16 [4096, 16384], P('task', 'tile')
All inputs are finite; a program needn't handle non-finite values.
Results may differ from a plain program's by a relative error of at most 0.0025.
Values may be sent and summed in bfloat16 or wider, within the bound.
A program may use at most 64 MiB of HBM per device.

v0:
```python
import jax
import jax.numpy as jnp
from jax import lax
from jax.sharding import PartitionSpec as P

NEWTON = 5


HIGH = lax.Precision.HIGHEST


def column_gram(matrix):
    return lax.dot_general(
        matrix, matrix, (((0,), (0,)), ((), ())), precision=HIGH, preferred_element_type=jnp.float32
    )


def triangular_apply(factor, matrix):
    return lax.linalg.triangular_solve(
        factor, matrix, left_side=False, lower=True, transpose_a=True
    )


def transposed_product(weights, basis):
    return lax.dot_general(
        weights,
        basis.astype(jnp.bfloat16),
        (((0,), (0,)), ((), ())),
        preferred_element_type=jnp.float32,
    )


def column_basis(weights, operand):
    partial_sum = jnp.dot(weights, operand, preferred_element_type=jnp.float32)
    summed = lax.psum(partial_sum, "tile")
    factor = jnp.linalg.cholesky(column_gram(summed))
    return triangular_apply(factor, summed)


def row_basis(weights, basis):
    projected = transposed_product(weights, basis)
    gram_total = lax.psum(column_gram(projected), "tile")
    factor = jnp.linalg.cholesky(gram_total)
    return (triangular_apply(factor, projected), factor)


def block_core(lowers):
    count = lowers.shape[0]
    rank = lowers.shape[1]
    identity = jnp.eye(count, dtype=jnp.float32)
    blocks = identity[:, None, :, None] * lowers[:, :, None, :]
    return blocks.reshape(count * rank, count * rank)


def whitening(gram_matrix):
    scale = jnp.sqrt(jnp.sum(gram_matrix * gram_matrix))
    identity = jnp.eye(gram_matrix.shape[0], dtype=jnp.float32)
    approx = gram_matrix / scale
    inverse = identity
    for newton_step in range(NEWTON):
        middle = 0.5 * (3.0 * identity - jnp.dot(inverse, approx, precision=HIGH))
        approx = jnp.dot(approx, middle, precision=HIGH)
        inverse = jnp.dot(middle, inverse, precision=HIGH)
    return inverse / jnp.sqrt(scale)


def on_device(deltas, sketches):
    weights = deltas[0]
    sketch = sketches[0]
    rank = sketch.shape[1]
    first_basis = column_basis(weights, sketch)
    power_basis, unused = row_basis(weights, first_basis)
    left_basis = column_basis(weights, power_basis.astype(jnp.bfloat16))
    right_basis, lower_factor = row_basis(weights, left_basis)
    left_rows = lax.all_to_all(left_basis, "task", split_axis=0, concat_axis=1, tiled=True)
    right_cols, lower_stack = (
        lax.all_gather(right_basis, "task", axis=1, tiled=True),
        lax.all_gather(lower_factor, "task", axis=0, tiled=True),
    )
    task_count = lower_stack.shape[0] // rank
    blocks = block_core(lower_stack.reshape(task_count, rank, rank))
    gram_left = lax.psum(column_gram(left_rows), "task")
    gram_right = lax.psum(column_gram(right_cols), "tile")
    left_white = whitening(gram_left)
    right_white = whitening(gram_right)
    middle = jnp.dot(jnp.dot(left_white, blocks, precision=HIGH), right_white, precision=HIGH)
    scaled_left = jnp.dot(left_rows, middle, precision=HIGH)
    merged = lax.dot_general(
        scaled_left,
        right_cols,
        (((1,), (1,)), ((), ())),
        precision=HIGH,
        preferred_element_type=jnp.float32,
    )
    return merged.astype(jnp.bfloat16)


def solution(mesh):
    in_specs = (P("task", None, "tile"), P("task", "tile", None))
    out_specs = P("task", "tile")
    return jax.shard_map(
        on_device, mesh=mesh, in_specs=in_specs, out_specs=out_specs, check_vma=False
    )
```

profile of v0, /device:TPU:1, one launch (start us, length us, event | category | flops | bytes accessed | tf_op | source)
XLA Modules:
  0.0 831.2 jit_solution(2220496298141359555)
XLA Ops:
  6.5 0.7 copy-done
  7.3 4.1 fusion.6
  11.4 156.6 %all-reduce.5.cloned.1.call-done = f32[4096,16]{0,1:T(8,128)} async-done(((f32[4096,16]{0,1:T(8,128)}), f32[4096,16]{0,1:T(8,128)}) %all-reduce.5.cloned.1.call-update) | async-done | bytes 262160 | tf_op jit(solution)/shard_map/psum | solution.py:35
  168.1 1.5 fusion.46
  169.6 1.5 cholesky.74
  171.1 0.6 compare_reduce_fusion.3
  171.8 0.6 fusion.26
  172.4 1.2 custom-call.10
  173.7 1.4 fusion
  175.0 2.8 fusion.4
  178.0 59.2 %psum.43 = f32[16,16]{0,1:T(8,128)S(1)} all-reduce(f32[16,16]{0,1:T(8,128)S(1)} %fusion.47), channel_id=1, replica_groups=mesh['task'=16,'tile'=32] {'tile'}, use_global_device_ids=true, to_apply=%region_3.6 | all-reduce | flops 256 | bytes 2048 | tf_op jit(solution)/shard_map/psum | solution.py:42
  237.3 1.5 cholesky.85
  238.8 0.6 compare_reduce_fusion.2
  239.5 0.6 fusion.27
  240.1 1.2 custom-call.11
  241.6 4.1 convolution_bitcast_fusion
  245.7 163.2 %all-reduce.7.cloned.1.call-done = f32[4096,16]{0,1:T(8,128)} async-done(((f32[4096,16]{0,1:T(8,128)}), f32[4096,16]{0,1:T(8,128)}) %all-reduce.7.cloned.1.call-update) | async-done | bytes 262160 | tf_op jit(solution)/shard_map/psum | solution.py:35
  408.9 1.5 fusion.48
  410.5 1.5 cholesky.96
  412.0 0.6 compare_reduce_fusion.1
  412.6 0.6 fusion.28
  413.3 1.2 custom-call.12
  414.5 1.4 fusion.31
  415.9 2.8 fusion.1
  418.7 0.7 copy.20
  419.5 11.8 %all-to-all-start = ((f32[16,256,16]{1,2,0:T(8,128)}), f32[16,256,16]{1,2,0:T(8,128)S(1)}, u32[]{:S(2)}, u32[]{:S(2)}) async-start(f32[16,256,16]{1,2,0:T(8,128)} %bitcast.159), calls=%async_computation | async-start | bytes 524288 | tf_op jit(solution)/shard_map/all_to_all | solution.py:75
  431.5 59.4 %psum.46 = f32[16,16]{0,1:T(8,128)S(1)} all-reduce(f32[16,16]{0,1:T(8,128)S(1)} %fusion.56), channel_id=1, replica_groups=mesh['task'=16,'tile'=32] {'tile'}, use_global_device_ids=true, to_apply=%region_7.11 | all-reduce | flops 256 | bytes 2048 | tf_op jit(solution)/shard_map/psum | solution.py:42
  491.0 1.5 cholesky.107
  492.5 0.7 compare_reduce_fusion
  493.2 0.7 select_bitcast_fusion
  493.9 31.6 %all_gather.6 = f32[256,16]{1,0:T(8,128)S(1)} all-gather(f32[16,16]{1,0:T(8,128)S(1)} %get-tuple-element.8), channel_id=1, replica_groups=mesh['task'=16,'tile'=32] {'task'}, dimensions={0}, use_global_device_ids=true | all-gather | bytes 17408 | tf_op jit(solution)/shard_map/all_gather | solution.py:78
  525.5 1.2 custom-call.13
  526.9 16.7 %all_gather.7 = f32[512,256]{0,1:T(8,128)S(1)} all-gather(f32[512,16]{0,1:T(8,128)S(1)} %convolution_bitcast_fusion.2), channel_id=1, replica_groups=mesh['task'=16,'tile'=32] {'task'}, dimensions={1}, use_global_device_ids=true | all-gather | bytes 557056 | tf_op jit(solution)/shard_map/all_gather | solution.py:77
  543.6 1.3 fusion.58
  545.4 0.9 mul.96
  546.3 140.9 %all-reduce.11.cloned.1.call-done = f32[256,256]{1,0:T(8,128)} async-done(((f32[256,256]{1,0:T(8,128)}), f32[256,256]{1,0:T(8,128)}) %all-reduce.11.cloned.1.call-update) | async-done | bytes 262160 | tf_op jit(solution)/shard_map/psum | solution.py:83
  687.2 1.7 multiply_reduce_fusion
  689.6 1.3 fusion.12
  691.1 1.3 fusion.22
  693.6 0.4 fusion.10
  694.8 0.4 fusion.9
  696.4 1.1 fusion.49
  697.9 114.5 %all-reduce.9.cloned.1.call-done = f32[256,256]{1,0:T(8,128)} async-done(((f32[256,256]{1,0:T(8,128)}), f32[256,256]{1,0:T(8,128)}) %all-reduce.9.cloned.1.call-update) | async-done | bytes 262160 | tf_op jit(solution)/shard_map/psum | solution.py:82
  812.5 1.6 multiply_reduce_fusion.1
  814.8 1.3 fusion.17
  816.3 1.3 fusion.21
  822.8 0.6 fusion.66
  823.4 1.3 convolution_convert_fusion
  (52 shorter events, 10.7 us)
Async XLA Ops:
  6.5 0.7 copy-start
  6.5 161.5 %all-reduce.5.cloned.1.call-start = ((), (), s32[]{:S(2)}) async-start(), calls=%async_computation.1 | async-start | bytes 524288 | tf_op jit(solution)/shard_map/psum | solution.py:35
  11.4 397.6 %all-reduce.7.cloned.1.call-start = ((), (), s32[]{:S(2)}) async-start(), calls=%async_computation.2 | async-start | bytes 524288 | tf_op jit(solution)/shard_map/psum | solution.py:35
  419.5 276.9 %all-to-all-start = ((f32[16,256,16]{1,2,0:T(8,128)}), f32[16,256,16]{1,2,0:T(8,128)S(1)}, u32[]{:S(2)}, u32[]{:S(2)}) async-start(f32[16,256,16]{1,2,0:T(8,128)} %bitcast.159), calls=%async_computation | async-start | bytes 524288 | tf_op jit(solution)/shard_map/all_to_all | solution.py:75
  431.3 255.9 %all-reduce.11.cloned.1.call-start = ((), (), s32[]{:S(2)}) async-start(), calls=%async_computation.4 | async-start | bytes 524288 | tf_op jit(solution)/shard_map/psum | solution.py:83
  545.0 267.5 %all-reduce.9.cloned.1.call-start = ((), (), s32[]{:S(2)}) async-start(), calls=%async_computation.3 | async-start | bytes 524288 | tf_op jit(solution)/shard_map/psum | solution.py:82
Sparse Core Ops, SparseCore 0:
  11.5 156.5 all-reduce.4
  245.9 163.0 all-reduce.6
  545.1 142.0 all-reduce.10
  697.6 114.7 all-reduce.8
where the time goes:
time: 832 us; the launch traced here: 831 us
  waiting for transfers between devices  575 us (69%)
  blocking collectives  167 us (20%)
  matrix products  39.5 us (5%)
  other arithmetic  19.7 us (2%)
  between operations  14.9 us (2%)
  starting transfers between devices  12.1 us (1%)
    psum x2, waiting for transfers between devices, column_basis(): summed = lax.psum(partial_sum, 'tile')  320 us
    psum x1, waiting for transfers between devices, on_device(): gram_right = lax.psum(column_gram(right_cols), 'tile')  141 us
    psum x2, blocking collectives, row_basis(): gram_total = lax.psum(column_gram(projected), 'tile')  119 us
    psum x1, waiting for transfers between devices, on_device(): gram_left = lax.psum(column_gram(left_rows), 'task')  115 us
    all_gather x1, blocking collectives, on_device(): lax.all_gather(lower_factor, 'task', axis=0, tiled=True)  31.6 us
    all_gather x1, blocking collectives, on_device(): lax.all_gather(right_basis, 'task', axis=1, tiled=True)  16.7 us
  transfers between devices with their start and end apart: 5, of which 4 were waited for; matrix products, arithmetic and copies ran while one was open for 2% of the time, Pallas kernels for 0%

commit v1 on v0

v1 whole, which is shorter than its diff:
```python
import functools

import jax
import jax.numpy as jnp
from jax import lax
from jax.experimental import pallas as pl
from jax.experimental.pallas import tpu as pltpu
from jax.sharding import PartitionSpec as P

NEWTON = 5
RANK = 16
LANES = 128
RING_Z = 8
CORES = 2
CHUNKS = 8
MESH = pl.DeviceIdType.MESH
HIGH = lax.Precision.HIGHEST
F32 = jnp.float32
BF16 = jnp.bfloat16

NN = (((1,), (0,)), ((), ()))
NT = (((1,), (1,)), ((), ()))
TN = (((0,), (0,)), ((), ()))

SEMS = ("a1", "a2", "gx", "gz", "c1", "c2", "t1y", "t1c", "pm", "la", "ey", "ec",
        "f1l", "f2l", "f3ly", "f3lc", "f1r", "f2r", "f3ry", "f3rc")
SEM = {name: index for index, name in enumerate(SEMS)}


def dot(a, b, dims=NN):
    return lax.dot_general(a, b, dims, preferred_element_type=F32)


def dot_high(a, b, dims=NN):
    return lax.dot_general(a, b, dims, precision=HIGH, preferred_element_type=F32)


def split(x):
    high = x.astype(BF16)
    return high, (x - high.astype(F32)).astype(BF16)


def dot_split(a, b, dims=NN):
    return dot(a[0], b[0], dims) + (dot(a[0], b[1], dims) + dot(a[1], b[0], dims))


def rsqrt(x):
    r = lax.rsqrt(x)
    return r * (1.5 - 0.5 * x * r * r)


def cholesky(columns):
    columns = list(columns)
    scales = []
    for k in range(RANK):
        scale = rsqrt(columns[k][k : k + 1, :])
        scales.append(scale)
        columns[k] = columns[k] * scale
        for i in range(k + 1, RANK):
            columns[i] = columns[i] - columns[k][i : i + 1, :] * columns[k]
    return columns, scales


def lane_columns(gram):
    return [jnp.broadcast_to(gram[:, i : i + 1], (RANK, LANES)) for i in range(RANK)]


def forward_solve(factor, tiles):
    columns, scales = factor
    row = lax.broadcasted_iota(jnp.int32, (RANK, LANES), 0)
    tiles = list(tiles)
    for k in range(RANK):
        below = jnp.where(row > k, columns[k], 0.0)
        at = row == k
        for n, tile in enumerate(tiles):
            solved = tile[k : k + 1, :] * scales[k]
            tiles[n] = jnp.where(at, jnp.broadcast_to(solved, tile.shape), tile - below * solved)
    return tiles


def to_tiles(matrix):
    return [matrix[:, n : n + LANES] for n in range(0, matrix.shape[1], LANES)]


def whitening(gram_matrix, eye):
    size = gram_matrix.shape[0]
    scale = jnp.sqrt(jnp.sum(gram_matrix * gram_matrix, keepdims=True))
    approx = gram_matrix / scale
    inverse = None
    for step in range(NEWTON):
        approx_halves = split(approx)
        if step == 0:
            product = approx
        else:
            inverse_halves = split(inverse)
            product = dot_split(inverse_halves, approx_halves)
        middle = 0.5 * (3.0 * eye - product)
        middle_halves = split(middle)
        if step < NEWTON - 1:
            approx = dot_split(approx_halves, middle_halves)
        inverse = middle if step == 0 else dot_split(middle_halves, inverse_halves)
    return inverse / jnp.sqrt(scale)


def block_factors(gram_left, gram_right, size):
    tasks = size // RANK
    group = LANES // (2 * tasks)
    lane = lax.broadcasted_iota(jnp.int32, (RANK, size), 1)
    sub = lax.broadcasted_iota(jnp.int32, (RANK, size), 0)
    pick = lane % RANK == sub
    grams = (gram_left, gram_right)
    spread_row = lax.broadcasted_iota(jnp.int32, (size, LANES), 0) // RANK
    spread_lane = lax.broadcasted_iota(jnp.int32, (size, LANES), 1) // group
    total = None
    for side, gram in enumerate(grams):
        diagonal = jnp.zeros((RANK, size), F32)
        for b in range(tasks):
            diagonal = jnp.where(lane // RANK == b, gram[b * RANK : (b + 1) * RANK, :], diagonal)
        rows = [jnp.where(pick, jnp.broadcast_to(diagonal[i : i + 1, :], (RANK, size)), 0.0) for i in range(RANK)]
        stack = jnp.concatenate(rows, axis=0)
        spread = (spread_lane == spread_row + side * tasks).astype(F32)
        term = dot_high(stack, spread)
        total = term if total is None else total + term
    columns, scales = cholesky([total[i * RANK : (i + 1) * RANK, :] for i in range(RANK)])
    row = lax.broadcasted_iota(jnp.int32, (RANK, LANES), 0)
    inverse = [(row == i).astype(F32) for i in range(RANK)]
    for k in range(RANK):
        inverse[k] = inverse[k] * scales[k]
        for i in range(k + 1, RANK):
            inverse[i] = inverse[i] - columns[k][i : i + 1, :] * inverse[k]
    stack = jnp.concatenate(inverse, axis=0)
    back_lane = lax.broadcasted_iota(jnp.int32, (LANES, size), 0)
    back_col = lax.broadcasted_iota(jnp.int32, (LANES, size), 1) // RANK
    factors = []
    for side in range(2):
        back = (back_lane == (back_col + side * tasks) * group).astype(F32)
        wide = dot_high(stack, back)
        rows = [
            jnp.sum(jnp.where(pick, wide[i * RANK : (i + 1) * RANK, :], 0.0), axis=0, keepdims=True) for i in range(RANK)
        ]
        compact = jnp.concatenate(rows, axis=0)
        factors.append(jnp.concatenate([jnp.where(lane // RANK == b, compact, 0.0) for b in range(tasks)], axis=0))
    return factors


def kernel(tasks, tiles, d_hbm, sk_ref, out_ref, dv, a1s, a1r, a2, gxs, gxr, gzs, gzr, c1s, c1r, c2,
           sl, t1, la, e, f1ls, f1lr, f2l, f3l, f1rs, f1rr, f2r, f3r, load_sem, send_sem, recv_sem):
    me_t, me_j = lax.axis_index("task"), lax.axis_index("tile")
    ring_x = tiles // RING_Z
    ring_y = tasks // CORES
    x, z = me_j // RING_Z, me_j % RING_Z
    y, core = me_t // CORES, me_t % CORES
    rows = dv.shape[0]
    width = dv.shape[1]
    size = tasks * RANK
    per_task = tiles // tasks
    chunk = rows // CHUNKS

    loads = [
        pltpu.make_async_copy(
            d_hbm.at[0, pl.ds(n * chunk, chunk)], dv.at[pl.ds(n * chunk, chunk)], load_sem.at[n]
        )
        for n in range(CHUNKS)
    ]
    for load in loads:
        load.start()

    def tile_peer(k):
        return ((x + k // RING_Z) % ring_x) * RING_Z + (z + k % RING_Z) % RING_Z

    partner_t = me_j // per_task
    partner_j = me_t * per_task + me_j % per_task
    alone = partner_t == me_t
    twin = y * CORES + (1 - core)

    barrier = pltpu.get_barrier_semaphore()

    def greet(t, j):
        pl.semaphore_signal(barrier, inc=1, device_id=(t, j), device_id_type=MESH)

    def greet_tile(k, carry):
        greet(me_t, tile_peer(k))
        return carry

    def greet_y(k, carry):
        greet(((y + k) % ring_y) * CORES + core, me_j)
        return carry

    lax.fori_loop(1, tiles, greet_tile, 0)
    lax.fori_loop(1, ring_y, greet_y, 0)
    greet(twin, me_j)

    @pl.when(jnp.logical_not(alone))
    def _():
        greet(partner_t, partner_j)

    def send(src, dst, name, t, j):
        pltpu.make_async_remote_copy(
            src_ref=src, dst_ref=dst, send_sem=send_sem.at[SEM[name]], recv_sem=recv_sem.at[SEM[name]],
            device_id=(t, j), device_id_type=MESH,
        ).start()

    def wait(ref, count, sems, name):
        pltpu.make_async_copy(ref.at[pl.ds(0, count)], ref.at[pl.ds(0, count)], sems.at[SEM[name]]).wait()

    def to_tile(name, src, dst):
        def body(k, carry):
            j = tile_peer(k)
            send(src(j), dst(k), name, me_t, j)
            return carry

        lax.fori_loop(1, tiles, body, 0)

    def to_x(name, src, dst):
        def body(k, carry):
            send(src, dst.at[k], name, me_t, ((x + k) % ring_x) * RING_Z + z)
            return carry

        lax.fori_loop(1, ring_x, body, 0)

    def to_z(name, src, dst):
        def body(k, carry):
            send(src, dst.at[k], name, me_t, x * RING_Z + (z + k) % RING_Z)
            return carry

        lax.fori_loop(1, RING_Z, body, 0)

    def to_task(name, buf):
        send(buf.at[me_t], buf.at[me_t], name + "c", twin, me_j)

        def body(k, carry):
            send(buf.at[me_t], buf.at[me_t], name + "y", ((y + k) % ring_y) * CORES + core, me_j)
            return carry

        lax.fori_loop(1, ring_y, body, 0)

    def pass_on(name, buf):
        wait(buf, ring_y - 1, recv_sem, name + "y")

        def body(k, carry):
            t = ((y + k) % ring_y) * CORES + core
            send(buf.at[t], buf.at[t], name + "c", twin, me_j)
            return carry

        lax.fori_loop(1, ring_y, body, 0)

    sketch = sk_ref[0].astype(F32).T.astype(BF16)
    for n in range(CHUNKS):
        loads[n].wait()
        part = dot(sketch, dv[n * chunk : (n + 1) * chunk, :], NT).astype(BF16)
        for m in range(chunk // LANES):
            a1s[n * (chunk // LANES) + m] = part[:, m * LANES : (m + 1) * LANES]

    greeted = tiles - 1 + ring_y - 1 + 1 + jnp.where(alone, 0, 1)
    pl.semaphore_wait(barrier, greeted)

    to_tile("a1", lambda j: a1s.at[j], lambda k: a1r.at[k])
    wait(a1r, tiles - 1, recv_sem, "a1")
    total = a1s[me_j].astype(F32)
    for k in range(1, tiles):
        total += a1r[k].astype(F32)
    a2[me_j] = total.astype(BF16)
    to_tile("a2", lambda j: a2.at[me_j], lambda k: a2.at[me_j])
    wait(a2, tiles - 1, recv_sem, "a2")

    def project(blocks):
        basis = jnp.concatenate([blocks[j] for j in range(tiles)], axis=1)
        gram = dot(basis, basis, NT)
        product = jnp.zeros((RANK, width), F32)
        for n in range(CHUNKS):
            product += dot(basis[:, n * chunk : (n + 1) * chunk], dv[n * chunk : (n + 1) * chunk, :])
        factor = cholesky(lane_columns(gram))
        return jnp.concatenate(forward_solve(factor, to_tiles(product)), axis=1)

    power = project(a2)
    gram = dot_high(power, power, NT)
    gxs[...] = jnp.concatenate([gram, jnp.zeros((RANK, LANES - RANK), F32)], axis=1)
    to_x("gx", gxs, gxr)

    power_1 = power.astype(BF16)
    rest = power - power_1.astype(F32)
    power_2 = rest.astype(BF16)
    power_3 = (rest - power_2.astype(F32)).astype(BF16)
    parts = jnp.concatenate([power_1, power_2, power_3], axis=0)
    for n in range(CHUNKS):
        part = dot(parts, dv[n * chunk : (n + 1) * chunk, :], NT)
        part = part[:RANK] + (part[RANK : 2 * RANK] + part[2 * RANK :])
        for m in range(chunk // LANES):
            c1s[n * (chunk // LANES) + m] = part[:, m * LANES : (m + 1) * LANES]
    to_tile("c1", lambda j: c1s.at[j], lambda k: c1r.at[k])

    wait(gxr, ring_x - 1, recv_sem, "gx")
    total = gxs[...]
    for k in range(1, ring_x):
        total += gxr[k]
    gzs[...] = total
    to_z("gz", gzs, gzr)
    wait(gzr, RING_Z - 1, recv_sem, "gz")
    for k in range(1, RING_Z):
        total += gzr[k]
    power_factor = cholesky(lane_columns(total))

    wait(c1r, tiles - 1, recv_sem, "c1")
    total = c1s[me_j]
    for k in range(1, tiles):
        total += c1r[k]
    (left_slice,) = forward_solve(power_factor, [total])
    c2[me_j] = left_slice.astype(BF16)
    to_tile("c2", lambda j: c2.at[me_j], lambda k: c2.at[me_j])
    t1[me_t] = left_slice
    to_task("t1", t1)

    @pl.when(jnp.logical_not(alone))
    def _():
        sl[...] = left_slice
        send(sl, la.at[partner_j], "pm", partner_t, partner_j)

    @pl.when(alone)
    def _():
        la[me_j] = left_slice

    wait(c2, tiles - 1, recv_sem, "c2")
    e[me_t] = project(c2)
    to_task("e", e)

    @pl.when(jnp.logical_not(alone))
    def _():
        wait(la, 1, recv_sem, "pm")

    to_tile("la", lambda j: la.at[me_j], lambda k: la.at[me_j])

    def rows_out(block, buf):
        for h in range(size // LANES):
            for r in range(RANK):
                buf[h * RANK + r] = block[r : r + 1, h * LANES : (h + 1) * LANES]

    def reduced(name, own, received, gathered):
        wait(received, tiles - 1, recv_sem, name)
        total = own[me_j]
        for k in range(1, tiles):
            total += received[k]
        gathered[me_j] = total

    def block_row(gathered):
        return jnp.concatenate(
            [
                jnp.concatenate([gathered[h * RANK + r] for r in range(RANK)], axis=0)
                for h in range(size // LANES)
            ],
            axis=1,
        )

    pass_on("t1", t1)
    wait(t1, ring_y, recv_sem, "t1c")
    stacked = jnp.concatenate([t1[t] for t in range(tasks)], axis=0)
    rows_out(dot_high(t1[me_t], stacked, NT), f1ls)
    to_tile("f1l", lambda j: f1ls.at[j], lambda k: f1lr.at[k])

    pass_on("e", e)
    wait(e, ring_y, recv_sem, "ec")
    stacked = jnp.concatenate([e[t] for t in range(tasks)], axis=0)
    rows_out(dot_high(e[me_t], stacked, NT), f1rs)
    to_tile("f1r", lambda j: f1rs.at[j], lambda k: f1rr.at[k])

    reduced("f1l", f1ls, f1lr, f2l)
    to_tile("f2l", lambda j: f2l.at[me_j], lambda k: f2l.at[me_j])
    reduced("f1r", f1rs, f1rr, f2r)
    to_tile("f2r", lambda j: f2r.at[me_j], lambda k: f2r.at[me_j])

    wait(f2l, tiles - 1, recv_sem, "f2l")
    f3l[me_t] = block_row(f2l)
    to_task("f3l", f3l)
    wait(f2r, tiles - 1, recv_sem, "f2r")
    f3r[me_t] = block_row(f2r)
    to_task("f3r", f3r)
    pass_on("f3l", f3l)
    pass_on("f3r", f3r)
    wait(f3l, ring_y, recv_sem, "f3lc")
    wait(f3r, ring_y, recv_sem, "f3rc")

    gram_left = jnp.concatenate([f3l[t] for t in range(tasks)], axis=0)
    gram_right = jnp.concatenate([f3r[t] for t in range(tasks)], axis=0)
    row = lax.broadcasted_iota(jnp.int32, (size, size), 0)
    column = lax.broadcasted_iota(jnp.int32, (size, size), 1)
    eye = (row == column).astype(F32)
    left_inverse, right_inverse = block_factors(gram_left, gram_right, size)
    left_halves, right_halves = split(left_inverse), split(right_inverse)
    cores = jnp.where(row // RANK == column // RANK, gram_right, 0.0)
    cores = dot_split(split(cores), right_halves, NT)
    gram_left = dot_split(split(dot_split(left_halves, split(gram_left))), left_halves, NT)
    gram_right = dot_split(split(dot_split(right_halves, split(gram_right))), right_halves, NT)
    left_white = whitening(gram_left, eye)
    right_white = whitening(gram_right, eye)
    middle = dot_split(split(dot_split(split(left_white), split(cores))), split(right_white))

    wait(la, tiles - 1, recv_sem, "la")
    left_rows = jnp.concatenate(
        [
            jnp.concatenate([la[t * per_task + b] for b in range(per_task)], axis=1)
            for t in range(tasks)
        ],
        axis=0,
    )
    right = dot_split(right_halves, split(stacked))
    left = dot_split(left_halves, split(left_rows))
    scaled = dot_split(split(left), split(middle), TN)
    out_ref[...] = dot_split(split(scaled), split(right)).astype(BF16)

    for name, ref, count in (
        ("a1", a1s, tiles - 1), ("a2", a2, tiles - 1), ("gx", gxr, ring_x - 1), ("gz", gzr, RING_Z - 1),
        ("c1", c1s, tiles - 1), ("c2", c2, tiles - 1), ("t1y", t1, ring_y - 1), ("t1c", t1, ring_y),
        ("la", la, tiles - 1), ("ey", e, ring_y - 1), ("ec", e, ring_y),
        ("f1l", f1ls, tiles - 1), ("f2l", f2l, tiles - 1), ("f3ly", f3l, ring_y - 1), ("f3lc", f3l, ring_y),
        ("f1r", f1rs, tiles - 1), ("f2r", f2r, tiles - 1), ("f3ry", f3r, ring_y - 1), ("f3rc", f3r, ring_y),
    ):
        wait(ref, count, send_sem, name)

    @pl.when(jnp.logical_not(alone))
    def _():
        wait(la, 1, send_sem, "pm")


def on_device(tasks, tiles, deltas, sketches):
    rows, width = deltas.shape[1:]
    size = tasks * RANK
    pieces = (tiles, 1, LANES)
    block = (tiles, RANK, LANES)
    ring_x = tiles // RING_Z
    return pl.pallas_call(
        functools.partial(kernel, tasks, tiles),
        out_shape=jax.ShapeDtypeStruct((rows // tasks, width), BF16),
        in_specs=[pl.BlockSpec(memory_space=pl.ANY), pl.BlockSpec(memory_space=pltpu.VMEM)],
        out_specs=pl.BlockSpec(memory_space=pltpu.VMEM),
        scratch_shapes=[
            pltpu.VMEM((rows, width), BF16),
            pltpu.VMEM(block, BF16), pltpu.VMEM(block, BF16), pltpu.VMEM(block, BF16),
            pltpu.VMEM((RANK, LANES), F32), pltpu.VMEM((ring_x, RANK, LANES), F32),
            pltpu.VMEM((RANK, LANES), F32), pltpu.VMEM((RING_Z, RANK, LANES), F32),
            pltpu.VMEM(block, F32), pltpu.VMEM(block, F32), pltpu.VMEM(block, BF16),
            pltpu.VMEM((RANK, LANES), F32), pltpu.VMEM((tasks, RANK, LANES), F32), pltpu.VMEM(block, F32),
            pltpu.VMEM((tasks, RANK, width), F32),
            pltpu.VMEM(pieces, F32), pltpu.VMEM(pieces, F32), pltpu.VMEM(pieces, F32),
            pltpu.VMEM((tasks, RANK, size), F32),
            pltpu.VMEM(pieces, F32), pltpu.VMEM(pieces, F32), pltpu.VMEM(pieces, F32),
            pltpu.VMEM((tasks, RANK, size), F32),
            pltpu.SemaphoreType.DMA((CHUNKS,)),
            pltpu.SemaphoreType.DMA((len(SEMS),)),
            pltpu.SemaphoreType.DMA((len(SEMS),)),
        ],
        compiler_params=pltpu.CompilerParams(
            collective_id=0, has_side_effects=True, vmem_limit_bytes=48 * 2**20
        ),
    )(deltas, sketches)


def solution(mesh):
    tasks, tiles = mesh.shape["task"], mesh.shape["tile"]
    return jax.shard_map(
        functools.partial(on_device, tasks, tiles),
        mesh=mesh,
        in_specs=(P("task", None, "tile"), P("task", "tile", None)),
        out_specs=P("task", "tile"),
        check_vma=False,
    )
```

time: 832 us -> 91.6 us (0.11)
  waiting for transfers between devices: 575 us -> 0 us
  blocking collectives: 167 us -> 0 us
  Pallas kernels: 0 us -> 87.7 us
  matrix products: 39.5 us -> 0 us
  other arithmetic: 19.7 us -> 0 us
  between operations: 14.9 us -> 0.02 us
  starting transfers between devices: 12.1 us -> 0 us
    psum x4 -> x0, waiting for transfers between devices: 575 us -> none  [the longest x2 320 us: column_basis(): summed = lax.psum(partial_sum, 'tile')]
    psum x2 -> x0, blocking collectives: 119 us -> none  [row_basis(): gram_total = lax.psum(column_gram(projected), 'tile')]
    pallas_call x0 -> x1, Pallas kernels: none -> 87.7 us  [on_device(): pl.pallas_call(functools.partial(kernel, tasks, tiles), out_shape=jax.Sha...]
    all_gather x2 -> x0, blocking collectives: 48.3 us -> none  [the longest x1 31.6 us: on_device(): lax.all_gather(lower_factor, 'task', axis=0, tiled=True)]
    dot_general x42 -> x0, matrix products: 36.3 us -> none  [the longest x2 8.21 us: column_basis(): partial_sum = jnp.dot(weights, operand, preferred_element_type=jnp.float32)]
    another operation x20 -> x0, other arithmetic: 16.2 us -> none  [the longest x8 7.55 us: triangular_apply(): lax.linalg.triangular_solve(factor, matrix, left_side=False, lower=True,...]
    all_to_all x1 -> x0, starting transfers between devices: 11.8 us -> none  [on_device(): lax.all_to_all(left_basis, 'task', split_axis=0, concat_axis=1, tiled=True)]
  transfers between devices with their start and end apart: 5 -> 0, of which waited for: 4 -> 0; matrix products, arithmetic and copies ran while one was open for 2% -> 0% of each run, Pallas kernels for 0% -> 0%
where the time goes in v1:
time: 91.6 us; the launch traced here: 91.4 us
  Pallas kernels  87.7 us (96%)
  local copies, waits for them, and re-layouts  3.73 us (4%)
    pallas_call x1, Pallas kernels, on_device(): pl.pallas_call(functools.partial(kernel, tasks, tiles), out_shape=jax.Sha...  87.7 us
    unnamed x4, local copies, waits for them, and re-layouts  3.73 us

profile of v1, /device:TPU:1, one launch (start us, length us, event | category | flops | bytes accessed | tf_op | source)
XLA Modules:
  0.0 91.4 jit_solution(15860682255955539429)
XLA Ops:
  0.0 0.8 copy.3.sk_ref
  0.8 0.0 copy-start
  0.9 2.2 %copy-done = bf16[1,4096,512]{2,1,0:T(8,128)(2,1)S(1)} copy-done((bf16[1,4096,512]{2,1,0:T(8,128)(2,1)S(1)}, bf16[1,4096,512]{2,1,0:T(8,128)(2,1)}, u32[]{:S(2)}) %copy-start) | copy-done | bytes 4194328
  3.0 87.7 %shard_map.28 = bf16[256,512]{1,0:T(8,128)(2,1)S(1)} custom-call(bf16[1,4096,512]{2,1,0:T(8,128)(2,1)S(1)} %copy-done, bf16[1,512,16]{2,1,0:T(8,128)(2,1)S(1)} %copy.3.sk_ref), custom_call_target="tpu_custom_call" | custom-call | tf_op jit(solution)/shard_map/pallas_call | solution.py:429
  90.7 0.7 copy.5
Async XLA Ops:
  0.8 2.2 %copy-start = (bf16[1,4096,512]{2,1,0:T(8,128)(2,1)S(1)}, bf16[1,4096,512]{2,1,0:T(8,128)(2,1)}, u32[]{:S(2)}) copy-start(bf16[1,4096,512]{2,1,0:T(8,128)(2,1)} %d_hbm.1) | copy-start | bytes 12582916

commit v2 on v1

v2 whole, which is shorter than its diff:
```python
import functools

import jax
import jax.numpy as jnp
from jax import lax
from jax.experimental import pallas as pl
from jax.experimental.pallas import tpu as pltpu
from jax.sharding import PartitionSpec as P

NEWTON = 5
RANK = 16
LANES = 128
RING_X, RING_Z = 4, 8
RING_Y, CORES = 8, 2
CHUNKS = 8
MESH = pl.DeviceIdType.MESH
HIGH = lax.Precision.HIGHEST
F32 = jnp.float32
BF16 = jnp.bfloat16

NN = (((1,), (0,)), ((), ()))
NT = (((1,), (1,)), ((), ()))
TN = (((0,), (0,)), ((), ()))

SEMS = ("a1", "a2", "gp", "c1", "c1x", "c2", "gl", "t1y", "t1c", "pm", "la", "ey", "ec", "ely", "elc", "gr",
        "dl", "dr", "rl", "al", "rr", "ar")
SEM = {name: index for index, name in enumerate(SEMS)}


def around(step, ring):
    return min(step, ring - step)


TILE_STEPS = sorted(
    ((a, b) for a in range(RING_X) for b in range(RING_Z) if (a, b) != (0, 0)),
    key=lambda step: -around(step[0], RING_X) - around(step[1], RING_Z),
)
Y_STEPS = sorted(range(1, RING_Y), key=lambda step: -around(step, RING_Y))


def dot(a, b, dims=NN):
    return lax.dot_general(a, b, dims, preferred_element_type=F32)


def dot_high(a, b, dims=NN):
    return lax.dot_general(a, b, dims, precision=HIGH, preferred_element_type=F32)


def split(x):
    high = x.astype(BF16)
    return high, (x - high.astype(F32)).astype(BF16)


def dot_split(a, b, dims=NN):
    return dot(a[0], b[0], dims) + (dot(a[0], b[1], dims) + dot(a[1], b[0], dims))


def rsqrt(x):
    r = lax.rsqrt(x)
    return r * (1.5 - 0.5 * x * r * r)


def cholesky(columns):
    columns = list(columns)
    scales = []
    for k in range(RANK):
        scale = rsqrt(columns[k][k : k + 1, :])
        scales.append(scale)
        columns[k] = columns[k] * scale
        for i in range(k + 1, RANK):
            columns[i] = columns[i] - columns[k][i : i + 1, :] * columns[k]
    return columns, scales


def lane_columns(gram):
    return [jnp.broadcast_to(gram[:, i : i + 1], (RANK, LANES)) for i in range(RANK)]


def forward_solve(factor, tiles):
    columns, scales = factor
    row = rows_of((RANK, LANES))
    tiles = list(tiles)
    for k in range(RANK):
        below = jnp.where(row > k, columns[k], 0.0)
        at = row == k
        for n, tile in enumerate(tiles):
            solved = tile[k : k + 1, :] * scales[k]
            tiles[n] = jnp.where(at, jnp.broadcast_to(solved, tile.shape), tile - below * solved)
    return tiles


def to_tiles(matrix):
    return [matrix[:, n : n + LANES] for n in range(0, matrix.shape[1], LANES)]


def whitening(gram_matrix, eye):
    size = gram_matrix.shape[0]
    scale = jnp.sqrt(jnp.sum(gram_matrix * gram_matrix, keepdims=True))
    approx = gram_matrix / scale
    inverse = None
    for step in range(NEWTON):
        approx_halves = split(approx)
        if step == 0:
            product = approx
        else:
            inverse_halves = split(inverse)
            product = dot_split(inverse_halves, approx_halves)
        middle = 0.5 * (3.0 * eye - product)
        middle_halves = split(middle)
        if step < NEWTON - 1:
            approx = dot_split(approx_halves, middle_halves)
        inverse = middle if step == 0 else dot_split(middle_halves, inverse_halves)
    return inverse / jnp.sqrt(scale)


def lanes_of(shape):
    return lax.broadcasted_iota(jnp.int32, shape, 1)


def rows_of(shape):
    return lax.broadcasted_iota(jnp.int32, shape, 0)


def repeat_lanes(wide):
    for shift in (RANK, 2 * RANK, 4 * RANK):
        wide = wide + pltpu.roll(wide, shift, 1)
    return wide


def pack(gram):
    shape = (RANK, LANES)
    wide = repeat_lanes(jnp.concatenate([gram, jnp.zeros((RANK, LANES - RANK), F32)], axis=1))
    wide = jnp.where(lanes_of(shape) // RANK == rows_of(shape) % 8, wide, 0.0)
    return jnp.concatenate(
        [jnp.sum(wide[:8], axis=0, keepdims=True), jnp.sum(wide[8:], axis=0, keepdims=True)], axis=0
    )


def unpack(packed):
    shape = (RANK, LANES)
    wide = jnp.where(rows_of(shape) < 8, packed[0:1, :], packed[1:2, :])
    return repeat_lanes(jnp.where(lanes_of(shape) // RANK == rows_of(shape) % 8, wide, 0.0))


def side_by_side(packed):
    shape = (RANK, LANES)
    halves = []
    for h in range(2):
        half = jnp.zeros(shape, F32)
        for b in range(8):
            half = jnp.where(lanes_of(shape) // RANK == b, unpack(packed[8 * h + b]), half)
        halves.append(half)
    return jnp.concatenate(halves, axis=1)


def block_diagonal(blocks):
    tasks = blocks.shape[1] // RANK
    lane = lanes_of(blocks.shape)
    return jnp.concatenate([jnp.where(lane // RANK == b, blocks, 0.0) for b in range(tasks)], axis=0)


def fold(gram):
    shape = (LANES, LANES)
    first = jnp.where(rows_of(shape) >= lanes_of(shape), gram[:LANES, :LANES], gram[LANES:, LANES:])
    return jnp.concatenate([first, gram[:LANES, LANES:]], axis=0)


def unfold(folded, blocks):
    shape = (LANES, LANES)
    first, cross = folded[:LANES], folded[LANES:]
    turned = first.T
    lower = rows_of(shape) >= lanes_of(shape)
    top = jnp.concatenate([jnp.where(lower, first, turned), cross], axis=1)
    bottom = jnp.concatenate([cross.T, jnp.where(lower, turned, first)], axis=1)
    gram = jnp.concatenate([top, bottom], axis=0)
    return jnp.where(rows_of(gram.shape) // RANK == lanes_of(gram.shape) // RANK, blocks, gram)


def three(x):
    first = x.astype(BF16)
    rest = x - first.astype(F32)
    second = rest.astype(BF16)
    return first, second, (rest - second.astype(F32)).astype(BF16)


def dot_ones(a, ones):
    first, second, third = three(a)
    return dot(first, ones) + (dot(second, ones) + dot(third, ones))


def block_factors(sides):
    size = sides[0].shape[1]
    tasks = size // RANK
    group = LANES // (2 * tasks)
    lane, sub = lanes_of((RANK, size)), rows_of((RANK, size))
    pick = lane % RANK == sub
    spread_row = rows_of((size, LANES)) // RANK
    spread_lane = lanes_of((size, LANES)) // group
    total = None
    for side, blocks in enumerate(sides):
        rows = [jnp.where(pick, jnp.broadcast_to(blocks[i : i + 1, :], (RANK, size)), 0.0) for i in range(RANK)]
        spread = (spread_lane == spread_row + side * tasks).astype(F32).astype(BF16)
        term = dot_ones(jnp.concatenate(rows, axis=0), spread)
        total = term if total is None else total + term
    columns, scales = cholesky([total[i * RANK : (i + 1) * RANK, :] for i in range(RANK)])
    row = rows_of((RANK, LANES))
    inverse = [(row == i).astype(F32) for i in range(RANK)]
    for k in range(RANK):
        inverse[k] = inverse[k] * scales[k]
        for i in range(k + 1, RANK):
            inverse[i] = inverse[i] - columns[k][i : i + 1, :] * inverse[k]
    stack = jnp.concatenate(inverse, axis=0)
    back_lane = rows_of((LANES, size))
    back_col = lanes_of((LANES, size)) // RANK
    factors = []
    for side in range(2):
        back = (back_lane == (back_col + side * tasks) * group).astype(F32).astype(BF16)
        wide = dot_ones(stack, back)
        rows = [
            jnp.sum(jnp.where(pick, wide[i * RANK : (i + 1) * RANK, :], 0.0), axis=0, keepdims=True) for i in range(RANK)
        ]
        factors.append(block_diagonal(jnp.concatenate(rows, axis=0)))
    return factors


def kernel(d_hbm, sk_hbm, out_ref, dv, skv, a1s, a1r, a2, gps, gpr, c1s, c1r, c1xs, c1xr, c2,
           gls, glr, grs, grr, dl, dr, sl, t1, la, eh, el, wls, wlr, wlg, wrs, wrr, wrg,
           load_sem, send_sem, recv_sem):
    me_t, me_j = lax.axis_index("task"), lax.axis_index("tile")
    x, z = me_j // RING_Z, me_j % RING_Z
    y, core = me_t // CORES, me_t % CORES
    rows, width = dv.shape
    tiles, tasks = la.shape[0], t1.shape[0]
    per_task = tiles // tasks
    chunk = rows // CHUNKS

    sketch_load = pltpu.make_async_copy(sk_hbm.at[0], skv, load_sem.at[CHUNKS])
    sketch_load.start()
    loads = [
        pltpu.make_async_copy(
            d_hbm.at[0, pl.ds(n * chunk, chunk)], dv.at[pl.ds(n * chunk, chunk)], load_sem.at[n]
        )
        for n in range(CHUNKS)
    ]
    for load in loads:
        load.start()

    xs = [((x + a) % RING_X) * RING_Z for a in range(RING_X)]
    zs = [(z + b) % RING_Z for b in range(RING_Z)]
    ys = [((y + c) % RING_Y) * CORES for c in range(RING_Y)]
    twin = y * CORES + (1 - core)
    partner_t = me_j // per_task
    partner_j = me_t * per_task + me_j % per_task
    alone = partner_t == me_t

    barrier = pltpu.get_barrier_semaphore()

    def greet(t, j):
        pl.semaphore_signal(barrier, inc=1, device_id=(t, j), device_id_type=MESH)

    for a, b in TILE_STEPS:
        greet(me_t, xs[a] + zs[b])
    for c in Y_STEPS:
        greet(ys[c] + core, me_j)
        greet(ys[c] + (1 - core), me_j)
    greet(twin, me_j)

    @pl.when(jnp.logical_not(alone))
    def _():
        greet(partner_t, partner_j)

    def send(src, dst, name, t, j):
        pltpu.make_async_remote_copy(
            src_ref=src, dst_ref=dst, send_sem=send_sem.at[SEM[name]], recv_sem=recv_sem.at[SEM[name]],
            device_id=(t, j), device_id_type=MESH,
        ).start()

    def wait(ref, count, sems, name):
        pltpu.make_async_copy(ref.at[pl.ds(0, count)], ref.at[pl.ds(0, count)], sems.at[SEM[name]]).wait()

    def scatter(name, src, dst):
        for a, b in TILE_STEPS:
            j = xs[a] + zs[b]
            send(src.at[j], dst.at[a * RING_Z + b], name, me_t, j)

    def to_each(name, src, dst):
        for a, b in TILE_STEPS:
            send(src, dst.at[a * RING_Z + b], name, me_t, xs[a] + zs[b])

    def gather(name, buf):
        for a, b in TILE_STEPS:
            send(buf.at[me_j], buf.at[me_j], name, me_t, xs[a] + zs[b])

    def received(name, own, buf):
        wait(buf, tiles - 1, recv_sem, name)
        total = own.astype(F32)
        for k in range(1, tiles):
            total += buf[k].astype(F32)
        return total

    def to_task(name, buf):
        for c in Y_STEPS:
            send(buf.at[me_t], buf.at[me_t], name + "y", ys[c] + core, me_j)
        send(buf.at[me_t], buf.at[me_t], name + "c", twin, me_j)

    def pass_on(name, buf):
        wait(buf, RING_Y - 1, recv_sem, name + "y")
        for c in Y_STEPS:
            t = ys[c] + core
            send(buf.at[t], buf.at[t], name + "c", twin, me_j)

    def to_task_direct(name, buf):
        for c in Y_STEPS:
            send(buf.at[me_t], buf.at[me_t], name, ys[c] + core, me_j)
            send(buf.at[me_t], buf.at[me_t], name, ys[c] + (1 - core), me_j)
        send(buf.at[me_t], buf.at[me_t], name, twin, me_j)

    def store_pieces(buf, matrix):
        for p in range(tiles):
            buf[p] = matrix[8 * p : 8 * p + 8, :]

    def pieces(buf):
        return jnp.concatenate([buf[p] for p in range(tiles)], axis=0)

    sketch_load.wait()
    sketch = skv[...]
    for n in range(CHUNKS):
        loads[n].wait()
        part = dot(sketch, dv[n * chunk : (n + 1) * chunk, :], NT).astype(BF16)
        for m in range(chunk // LANES):
            a1s[n * (chunk // LANES) + m] = part[:, m * LANES : (m + 1) * LANES]

    pl.semaphore_wait(barrier, tiles - 1 + tasks - 1 + jnp.where(alone, 0, 1))

    scatter("a1", a1s, a1r)
    a2[me_j] = received("a1", a1s[me_j], a1r).astype(BF16)
    gather("a2", a2)
    wait(a2, tiles - 1, recv_sem, "a2")

    def project(blocks):
        basis = jnp.concatenate([blocks[j] for j in range(tiles)], axis=1)
        gram = dot(basis, basis, NT)
        product = jnp.zeros((RANK, width), F32)
        for n in range(CHUNKS):
            product += dot(basis[:, n * chunk : (n + 1) * chunk], dv[n * chunk : (n + 1) * chunk, :])
        factor = cholesky(lane_columns(gram))
        return jnp.concatenate(forward_solve(factor, to_tiles(product)), axis=1)

    power = project(a2)
    gps[...] = pack(dot_high(power, power, NT))
    to_each("gp", gps, gpr)

    parts = jnp.concatenate(three(power), axis=0)
    for n in range(CHUNKS):
        part = dot(parts, dv[n * chunk : (n + 1) * chunk, :], NT)
        high, low = split(part[:RANK] + (part[RANK : 2 * RANK] + part[2 * RANK :]))
        for m in range(chunk // LANES):
            c1s[n * (chunk // LANES) + m] = high[:, m * LANES : (m + 1) * LANES]
            c1xs[n * (chunk // LANES) + m] = low[:, m * LANES : (m + 1) * LANES]
    scatter("c1", c1s, c1r)
    scatter("c1x", c1xs, c1xr)

    power_factor = cholesky(lane_columns(unpack(received("gp", gps[...], gpr))))
    high = received("c1", c1s[me_j], c1r)
    c2[me_j] = forward_solve(power_factor, [high])[0].astype(BF16)
    gather("c2", c2)

    low = received("c1x", c1xs[me_j], c1xr)
    (left_slice,) = forward_solve(power_factor, [high + low])
    sl[...] = left_slice
    t1[me_t] = left_slice
    gls[...] = pack(dot_high(left_slice, left_slice, NT))
    to_task("t1", t1)
    to_each("gl", gls, glr)

    @pl.when(jnp.logical_not(alone))
    def _():
        send(sl, la.at[partner_j], "pm", partner_t, partner_j)

    @pl.when(alone)
    def _():
        la[me_j] = sl[...]

    wait(c2, tiles - 1, recv_sem, "c2")
    right = project(c2)
    high, low = split(right)
    eh[me_t] = high
    to_task("e", eh)
    grs[...] = pack(dot_high(right, right, NT))
    to_each("gr", grs, grr)
    el[me_t] = low
    to_task("el", el)

    dl[me_t] = received("gl", gls[...], glr)
    to_task_direct("dl", dl)
    pass_on("t1", t1)
    wait(t1, RING_Y, recv_sem, "t1c")
    stacked = split(jnp.concatenate([t1[t] for t in range(tasks)], axis=0))
    store_pieces(wls, fold(dot_split(stacked, stacked, NT)))
    scatter("rl", wls, wlr)

    @pl.when(jnp.logical_not(alone))
    def _():
        wait(la, 1, recv_sem, "pm")

    gather("la", la)

    pass_on("e", eh)
    wait(eh, RING_Y, recv_sem, "ec")
    stacked = jnp.concatenate([eh[t] for t in range(tasks)], axis=0)
    store_pieces(wrs, fold(dot(stacked, stacked, NT)))
    scatter("rr", wrs, wrr)

    dr[me_t] = received("gr", grs[...], grr)
    to_task_direct("dr", dr)
    pass_on("el", el)
    wlg[me_j] = received("rl", wls[me_j], wlr)
    gather("al", wlg)
    wrg[me_j] = received("rr", wrs[me_j], wrr)
    gather("ar", wrg)

    size = tasks * RANK
    eye = (rows_of((size, size)) == lanes_of((size, size))).astype(F32)
    wait(dl, tasks - 1, recv_sem, "dl")
    wait(dr, tasks - 1, recv_sem, "dr")
    left_blocks, right_blocks = side_by_side(dl), side_by_side(dr)
    left_inverse, right_inverse = block_factors((left_blocks, right_blocks))
    left_blocks, right_blocks = block_diagonal(left_blocks), block_diagonal(right_blocks)
    left_inverse, right_inverse = split(left_inverse), split(right_inverse)
    core_turned = dot_split(right_inverse, split(right_blocks))

    def orthonormal_gram(inverse, gram):
        return dot_split(split(dot_split(inverse, split(gram))), inverse, NT)

    wait(wlg, tiles - 1, recv_sem, "al")
    left_white = whitening(orthonormal_gram(left_inverse, unfold(pieces(wlg), left_blocks)), eye)
    wait(la, tiles - 1, recv_sem, "la")
    left_rows = jnp.concatenate(
        [
            jnp.concatenate([la[t * per_task + b] for b in range(per_task)], axis=1)
            for t in range(tasks)
        ],
        axis=0,
    )
    left = dot_split(left_inverse, split(left_rows))
    scaled = dot_split(split(core_turned), split(dot_split(split(left_white), split(left))))
    wait(el, RING_Y, recv_sem, "elc")
    right = (stacked, jnp.concatenate([el[t] for t in range(tasks)], axis=0))
    right = dot_split(right_inverse, right)

    wait(wrg, tiles - 1, recv_sem, "ar")
    right_white = whitening(orthonormal_gram(right_inverse, unfold(pieces(wrg), right_blocks)), eye)
    scaled = dot_split(split(right_white), split(scaled))
    out_ref[...] = dot_split(split(scaled), split(right), TN).astype(BF16)

    for name, ref, count in (
        ("a1", a1s, tiles - 1), ("a2", a2, tiles - 1), ("gp", gpr, tiles - 1), ("c1", c1s, tiles - 1),
        ("c1x", c1xs, tiles - 1), ("c2", c2, tiles - 1), ("gl", glr, tiles - 1), ("gr", grr, tiles - 1),
        ("t1y", t1, RING_Y - 1), ("t1c", t1, RING_Y), ("la", la, tiles - 1), ("ey", eh, RING_Y - 1),
        ("ec", eh, RING_Y), ("ely", el, RING_Y - 1), ("elc", el, RING_Y), ("dl", dl, tasks - 1),
        ("dr", dr, tasks - 1), ("rl", wls, tiles - 1), ("al", wlg, tiles - 1), ("rr", wrs, tiles - 1),
        ("ar", wrg, tiles - 1),
    ):
        wait(ref, count, send_sem, name)

    @pl.when(jnp.logical_not(alone))
    def _():
        wait(la, 1, send_sem, "pm")


def on_device(deltas, sketches):
    rows, width = deltas.shape[1:]
    tasks, tiles = RING_Y * CORES, RING_X * RING_Z
    block = (tiles, RANK, LANES)
    half = pltpu.VMEM(block, BF16)
    gram_in = pltpu.VMEM((tiles, 2, LANES), F32)
    gram_own = pltpu.VMEM((2, LANES), F32)
    gram_all = pltpu.VMEM((tasks, 2, LANES), F32)
    piece = pltpu.VMEM((tiles, 8, LANES), F32)
    return pl.pallas_call(
        kernel,
        out_shape=jax.ShapeDtypeStruct((rows // tasks, width), BF16),
        in_specs=[pl.BlockSpec(memory_space=pltpu.HBM)] * 2,
        out_specs=pl.BlockSpec(memory_space=pltpu.VMEM),
        scratch_shapes=[
            pltpu.VMEM((rows, width), BF16), pltpu.VMEM((RANK, width), BF16),
            half, half, half, gram_own, gram_in,
            half, half, half, half, half,
            gram_own, gram_in, gram_own, gram_in, gram_all, gram_all,
            pltpu.VMEM((RANK, LANES), F32), pltpu.VMEM((tasks, RANK, LANES), F32), pltpu.VMEM(block, F32),
            pltpu.VMEM((tasks, RANK, width), BF16), pltpu.VMEM((tasks, RANK, width), BF16),
            piece, piece, piece, piece, piece, piece,
            pltpu.SemaphoreType.DMA((CHUNKS + 1,)),
            pltpu.SemaphoreType.DMA((len(SEMS),)),
            pltpu.SemaphoreType.DMA((len(SEMS),)),
        ],
        compiler_params=pltpu.CompilerParams(
            collective_id=0, has_side_effects=True, vmem_limit_bytes=60 * 2**20
        ),
    )(deltas, jnp.swapaxes(sketches, 1, 2))


def solution(mesh):
    return jax.shard_map(
        on_device,
        mesh=mesh,
        in_specs=(P("task", None, "tile"), P("task", "tile", None)),
        out_specs=P("task", "tile"),
        check_vma=False,
    )
```

time: 91.6 us -> 78.2 us (0.85)
  Pallas kernels: 87.7 us -> 76.3 us
  local copies, waits for them, and re-layouts: 3.73 us -> 1.67 us
    pallas_call x1, Pallas kernels: 87.7 us -> 76.3 us  [on_device(): pl.pallas_call(kernel, out_shape=jax.ShapeDtypeStruct((rows // tasks, wid...]
    unnamed x4 -> x1, local copies, waits for them, and re-layouts: 3.73 us -> 1.67 us
where the time goes in v2:
time: 78.2 us; the launch traced here: 78 us
  Pallas kernels  76.3 us (98%)
  local copies, waits for them, and re-layouts  1.67 us (2%)
    pallas_call x1, Pallas kernels, on_device(): pl.pallas_call(kernel, out_shape=jax.ShapeDtypeStruct((rows // tasks, wid...  76.3 us
    unnamed x1, local copies, waits for them, and re-layouts  1.67 us

profile of v2, /device:TPU:1, one launch (start us, length us, event | category | flops | bytes accessed | tf_op | source)
XLA Modules:
  0.0 78.0 jit_solution(9667465873732388762)
XLA Ops:
  0.0 76.3 %shard_map.28 = bf16[256,512]{1,0:T(8,128)(2,1)} custom-call(bf16[1,4096,512]{2,1,0:T(8,128)(2,1)} %d_hbm.1, bf16[1,16,512]{2,1,0:T(8,128)(2,1)} %bitcast.1), custom_call_target="tpu_custom_call" | custom-call | tf_op jit(solution)/shard_map/pallas_call | solution.py:480
  76.3 1.7 %copy.4 = bf16[256,512]{1,0:T(8,128)(2,1)} copy(bf16[256,512]{1,0:T(8,128)(2,1)} %shard_map.28) | data formatting | bytes 524288

commit v3 on v2

--- a/solution.py
+++ b/solution.py
@@ -22,8 +22,8 @@
 NT = (((1,), (1,)), ((), ()))
 TN = (((0,), (0,)), ((), ()))
 
-SEMS = ("a1", "a2", "gp", "c1", "c1x", "c2", "gl", "t1y", "t1c", "pm", "la", "ey", "ec", "ely", "elc", "gr",
-        "dl", "dr", "rl", "al", "rr", "ar")
+SEMS = ("a1", "a20", "a21", "a22", "a23", "gp", "c1", "c1x", "c20", "c21", "c22", "c23", "c2x", "gl", "t1y", "t1c",
+        "lh", "ll", "ey", "ec", "ely", "elc", "gr", "dl", "dr", "rl", "al", "rr", "ar")
 SEM = {name: index for index, name in enumerate(SEMS)}
 
 
@@ -35,7 +35,9 @@
     ((a, b) for a in range(RING_X) for b in range(RING_Z) if (a, b) != (0, 0)),
     key=lambda step: -around(step[0], RING_X) - around(step[1], RING_Z),
 )
+X_STEPS = sorted(range(RING_X), key=lambda step: -around(step, RING_X))
 Y_STEPS = sorted(range(1, RING_Y), key=lambda step: -around(step, RING_Y))
+Z_STEPS = sorted(range(RING_Z), key=lambda step: -around(step, RING_Z))
 
 
 def dot(a, b, dims=NN):
@@ -93,24 +95,20 @@
     return [matrix[:, n : n + LANES] for n in range(0, matrix.shape[1], LANES)]
 
 
-def whitening(gram_matrix, eye):
-    size = gram_matrix.shape[0]
-    scale = jnp.sqrt(jnp.sum(gram_matrix * gram_matrix, keepdims=True))
-    approx = gram_matrix / scale
-    inverse = None
+def whitened(gram, matrix):
+    size = gram.shape[0]
+    eye = (rows_of((size, size)) == lanes_of((size, size))).astype(F32)
+    squares = jnp.sum(gram * gram, keepdims=True)
+    scale = jnp.sqrt(squares)
+    product = gram / scale
     for step in range(NEWTON):
-        approx_halves = split(approx)
-        if step == 0:
-            product = approx
-        else:
-            inverse_halves = split(inverse)
-            product = dot_split(inverse_halves, approx_halves)
-        middle = 0.5 * (3.0 * eye - product)
-        middle_halves = split(middle)
+        halves = split(product)
         if step < NEWTON - 1:
-            approx = dot_split(approx_halves, middle_halves)
-        inverse = middle if step == 0 else dot_split(middle_halves, inverse_halves)
-    return inverse / jnp.sqrt(scale)
+            square = dot_split(halves, halves)
+            following = dot_split(halves, split(2.25 * eye - 1.5 * product + 0.25 * square))
+        matrix = dot_split(split(1.5 * eye - 0.5 * product), split(matrix))
+        product = following
+    return matrix / jnp.sqrt(scale)
 
 
 def lanes_of(shape):
@@ -224,15 +222,33 @@
 
 
 def kernel(d_hbm, sk_hbm, out_ref, dv, skv, a1s, a1r, a2, gps, gpr, c1s, c1r, c1xs, c1xr, c2,
-           gls, glr, grs, grr, dl, dr, sl, t1, la, eh, el, wls, wlr, wlg, wrs, wrr, wrg,
+           c2x, gls, glr, grs, grr, dl, dr, t1, lh, ll, eh, el, wls, wlr, wlg, wrs, wrr, wrg,
            load_sem, send_sem, recv_sem):
     me_t, me_j = lax.axis_index("task"), lax.axis_index("tile")
     x, z = me_j // RING_Z, me_j % RING_Z
     y, core = me_t // CORES, me_t % CORES
     rows, width = dv.shape
-    tiles, tasks = la.shape[0], t1.shape[0]
+    tiles, tasks = c2.shape[0], t1.shape[0]
     per_task = tiles // tasks
     chunk = rows // CHUNKS
+    run = RING_Z * LANES
+
+    xs = [((x + a) % RING_X) * RING_Z for a in range(RING_X)]
+    zs = [(z + b) % RING_Z for b in range(RING_Z)]
+    ys = [((y + c) % RING_Y) * CORES for c in range(RING_Y)]
+    twin = y * CORES + (1 - core)
+
+    barrier = pltpu.get_barrier_semaphore()
+
+    def greet(t, j):
+        pl.semaphore_signal(barrier, inc=1, device_id=(t, j), device_id_type=MESH)
+
+    for a, b in TILE_STEPS:
+        greet(me_t, xs[a] + zs[b])
+    for c in Y_STEPS:
+        greet(ys[c] + core, me_j)
+        greet(ys[c] + (1 - core), me_j)
+    greet(twin, me_j)
 
     sketch_load = pltpu.make_async_copy(sk_hbm.at[0], skv, load_sem.at[CHUNKS])
     sketch_load.start()
@@ -245,30 +261,6 @@
     for load in loads:
         load.start()
 
-    xs = [((x + a) % RING_X) * RING_Z for a in range(RING_X)]
-    zs = [(z + b) % RING_Z for b in range(RING_Z)]
-    ys = [((y + c) % RING_Y) * CORES for c in range(RING_Y)]
-    twin = y * CORES + (1 - core)
-    partner_t = me_j // per_task
-    partner_j = me_t * per_task + me_j % per_task
-    alone = partner_t == me_t
-
-    barrier = pltpu.get_barrier_semaphore()
-
-    def greet(t, j):
-        pl.semaphore_signal(barrier, inc=1, device_id=(t, j), device_id_type=MESH)
-
-    for a, b in TILE_STEPS:
-        greet(me_t, xs[a] + zs[b])
-    for c in Y_STEPS:
-        greet(ys[c] + core, me_j)
-        greet(ys[c] + (1 - core), me_j)
-    greet(twin, me_j)
-
-    @pl.when(jnp.logical_not(alone))
-    def _():
-        greet(partner_t, partner_j)
-
     def send(src, dst, name, t, j):
         pltpu.make_async_remote_copy(
             src_ref=src, dst_ref=dst, send_sem=send_sem.at[SEM[name]], recv_sem=recv_sem.at[SEM[name]],
@@ -290,6 +282,10 @@
     def gather(name, buf):
         for a, b in TILE_STEPS:
             send(buf.at[me_j], buf.at[me_j], name, me_t, xs[a] + zs[b])
+
+    def gather_groups(name, buf):
+        for a, b in TILE_STEPS:
+            send(buf.at[me_j], buf.at[me_j], name + str(-a % RING_X), me_t, xs[a] + zs[b])
 
     def received(name, own, buf):
         wait(buf, tiles - 1, recv_sem, name)
@@ -309,11 +305,9 @@
             t = ys[c] + core
             send(buf.at[t], buf.at[t], name + "c", twin, me_j)
 
-    def to_task_direct(name, buf):
-        for c in Y_STEPS:
-            send(buf.at[me_t], buf.at[me_t], name, ys[c] + core, me_j)
-            send(buf.at[me_t], buf.at[me_t], name, ys[c] + (1 - core), me_j)
-        send(buf.at[me_t], buf.at[me_t], name, twin, me_j)
+    def to_task_direct(name, src, dst):
+        for t in [ys[c] + other for c in Y_STEPS for other in (core, 1 - core)] + [twin]:
+            send(src(t), dst.at[me_t], name, t, me_j)
 
     def store_pieces(buf, matrix):
         for p in range(tiles):
@@ -330,59 +324,55 @@
         for m in range(chunk // LANES):
             a1s[n * (chunk // LANES) + m] = part[:, m * LANES : (m + 1) * LANES]
 
-    pl.semaphore_wait(barrier, tiles - 1 + tasks - 1 + jnp.where(alone, 0, 1))
+    pl.semaphore_wait(barrier, tiles - 1 + tasks - 1)
 
     scatter("a1", a1s, a1r)
     a2[me_j] = received("a1", a1s[me_j], a1r).astype(BF16)
-    gather("a2", a2)
-    wait(a2, tiles - 1, recv_sem, "a2")
-
-    def project(blocks):
-        basis = jnp.concatenate([blocks[j] for j in range(tiles)], axis=1)
-        gram = dot(basis, basis, NT)
+    gather_groups("a2", a2)
+
+    def project(name, blocks):
+        gram = jnp.zeros((RANK, RANK), F32)
         product = jnp.zeros((RANK, width), F32)
-        for n in range(CHUNKS):
-            product += dot(basis[:, n * chunk : (n + 1) * chunk], dv[n * chunk : (n + 1) * chunk, :])
+        for a in reversed(X_STEPS):
+            wait(blocks, RING_Z - (a == 0), recv_sem, name + str(a))
+            basis = jnp.concatenate([blocks[xs[a] + b] for b in range(RING_Z)], axis=1)
+            product += dot(basis, dv[pl.ds(pl.multiple_of(xs[a] * LANES, run), run), :])
+            gram += dot(basis, basis, NT)
         factor = cholesky(lane_columns(gram))
         return jnp.concatenate(forward_solve(factor, to_tiles(product)), axis=1)
 
-    power = project(a2)
+    power = project("a2", a2)
     gps[...] = pack(dot_high(power, power, NT))
-    to_each("gp", gps, gpr)
 
     parts = jnp.concatenate(three(power), axis=0)
-    for n in range(CHUNKS):
-        part = dot(parts, dv[n * chunk : (n + 1) * chunk, :], NT)
+    for n, a in enumerate(X_STEPS):
+        part = dot(parts, dv[pl.ds(pl.multiple_of(xs[a] * LANES, run), run), :], NT)
         high, low = split(part[:RANK] + (part[RANK : 2 * RANK] + part[2 * RANK :]))
-        for m in range(chunk // LANES):
-            c1s[n * (chunk // LANES) + m] = high[:, m * LANES : (m + 1) * LANES]
-            c1xs[n * (chunk // LANES) + m] = low[:, m * LANES : (m + 1) * LANES]
-    scatter("c1", c1s, c1r)
+        for b in range(RING_Z):
+            c1s[xs[a] + b] = high[:, b * LANES : (b + 1) * LANES]
+            c1xs[xs[a] + b] = low[:, b * LANES : (b + 1) * LANES]
+        for b in Z_STEPS:
+            if (a, b) != (0, 0):
+                send(c1s.at[xs[a] + zs[b]], c1r.at[a * RING_Z + b], "c1", me_t, xs[a] + zs[b])
+        if n == 0:
+            to_each("gp", gps, gpr)
     scatter("c1x", c1xs, c1xr)
 
     power_factor = cholesky(lane_columns(unpack(received("gp", gps[...], gpr))))
     high = received("c1", c1s[me_j], c1r)
     c2[me_j] = forward_solve(power_factor, [high])[0].astype(BF16)
-    gather("c2", c2)
+    gather_groups("c2", c2)
 
     low = received("c1x", c1xs[me_j], c1xr)
     (left_slice,) = forward_solve(power_factor, [high + low])
-    sl[...] = left_slice
+    c2x[me_j] = (left_slice - c2[me_j].astype(F32)).astype(BF16)
+    gather("c2x", c2x)
     t1[me_t] = left_slice
     gls[...] = pack(dot_high(left_slice, left_slice, NT))
     to_task("t1", t1)
     to_each("gl", gls, glr)
 
-    @pl.when(jnp.logical_not(alone))
-    def _():
-        send(sl, la.at[partner_j], "pm", partner_t, partner_j)
-
-    @pl.when(alone)
-    def _():
-        la[me_j] = sl[...]
-
-    wait(c2, tiles - 1, recv_sem, "c2")
-    right = project(c2)
+    right = project("c2", c2)
     high, low = split(right)
     eh[me_t] = high
     to_task("e", eh)
@@ -392,35 +382,32 @@
     to_task("el", el)
 
     dl[me_t] = received("gl", gls[...], glr)
-    to_task_direct("dl", dl)
+    to_task_direct("dl", lambda t: dl.at[me_t], dl)
     pass_on("t1", t1)
     wait(t1, RING_Y, recv_sem, "t1c")
     stacked = split(jnp.concatenate([t1[t] for t in range(tasks)], axis=0))
     store_pieces(wls, fold(dot_split(stacked, stacked, NT)))
     scatter("rl", wls, wlr)
 
-    @pl.when(jnp.logical_not(alone))
-    def _():
-        wait(la, 1, recv_sem, "pm")
-
-    gather("la", la)
-
     pass_on("e", eh)
     wait(eh, RING_Y, recv_sem, "ec")
     stacked = jnp.concatenate([eh[t] for t in range(tasks)], axis=0)
     store_pieces(wrs, fold(dot(stacked, stacked, NT)))
     scatter("rr", wrs, wrr)
 
+    wait(c2x, tiles - 1, recv_sem, "c2x")
+    for name, src, dst in (("lh", c2, lh), ("ll", c2x, ll)):
+        to_task_direct(name, lambda t: src.at[pl.ds(t * per_task, per_task)], dst)
+        dst[me_t] = src[pl.ds(me_t * per_task, per_task)]
+
     dr[me_t] = received("gr", grs[...], grr)
-    to_task_direct("dr", dr)
+    to_task_direct("dr", lambda t: dr.at[me_t], dr)
     pass_on("el", el)
     wlg[me_j] = received("rl", wls[me_j], wlr)
     gather("al", wlg)
     wrg[me_j] = received("rr", wrs[me_j], wrr)
     gather("ar", wrg)
 
-    size = tasks * RANK
-    eye = (rows_of((size, size)) == lanes_of((size, size))).astype(F32)
     wait(dl, tasks - 1, recv_sem, "dl")
     wait(dr, tasks - 1, recv_sem, "dr")
     left_blocks, right_blocks = side_by_side(dl), side_by_side(dr)
@@ -432,40 +419,38 @@
     def orthonormal_gram(inverse, gram):
         return dot_split(split(dot_split(inverse, split(gram))), inverse, NT)
 
+    def rows_of_bases(buf):
+        return jnp.concatenate(
+            [jnp.concatenate([buf[t, b] for b in range(per_task)], axis=1) for t in range(tasks)], axis=0
+        )
+
+    wait(lh, tasks - 1, recv_sem, "lh")
+    wait(ll, tasks - 1, recv_sem, "ll")
+    left = dot_split(left_inverse, (rows_of_bases(lh), rows_of_bases(ll)))
     wait(wlg, tiles - 1, recv_sem, "al")
-    left_white = whitening(orthonormal_gram(left_inverse, unfold(pieces(wlg), left_blocks)), eye)
-    wait(la, tiles - 1, recv_sem, "la")
-    left_rows = jnp.concatenate(
-        [
-            jnp.concatenate([la[t * per_task + b] for b in range(per_task)], axis=1)
-            for t in range(tasks)
-        ],
-        axis=0,
-    )
-    left = dot_split(left_inverse, split(left_rows))
-    scaled = dot_split(split(core_turned), split(dot_split(split(left_white), split(left))))
+    left_gram = orthonormal_gram(left_inverse, unfold(pieces(wlg), left_blocks))
+    scaled = dot_split(split(core_turned), split(whitened(left_gram, left)))
     wait(el, RING_Y, recv_sem, "elc")
     right = (stacked, jnp.concatenate([el[t] for t in range(tasks)], axis=0))
     right = dot_split(right_inverse, right)
 
     wait(wrg, tiles - 1, recv_sem, "ar")
-    right_white = whitening(orthonormal_gram(right_inverse, unfold(pieces(wrg), right_blocks)), eye)
-    scaled = dot_split(split(right_white), split(scaled))
+    right_gram = orthonormal_gram(right_inverse, unfold(pieces(wrg), right_blocks))
+    scaled = whitened(right_gram, scaled)
     out_ref[...] = dot_split(split(scaled), split(right), TN).astype(BF16)
 
     for name, ref, count in (
-        ("a1", a1s, tiles - 1), ("a2", a2, tiles - 1), ("gp", gpr, tiles - 1), ("c1", c1s, tiles - 1),
-        ("c1x", c1xs, tiles - 1), ("c2", c2, tiles - 1), ("gl", glr, tiles - 1), ("gr", grr, tiles - 1),
-        ("t1y", t1, RING_Y - 1), ("t1c", t1, RING_Y), ("la", la, tiles - 1), ("ey", eh, RING_Y - 1),
-        ("ec", eh, RING_Y), ("ely", el, RING_Y - 1), ("elc", el, RING_Y), ("dl", dl, tasks - 1),
-        ("dr", dr, tasks - 1), ("rl", wls, tiles - 1), ("al", wlg, tiles - 1), ("rr", wrs, tiles - 1),
-        ("ar", wrg, tiles - 1),
+        ("a1", a1s, tiles - 1), ("gp", gpr, tiles - 1), ("c1", c1s, tiles - 1), ("c1x", c1xs, tiles - 1),
+        ("c2x", c2x, tiles - 1), ("gl", glr, tiles - 1), ("gr", grr, tiles - 1),
+        ("t1y", t1, RING_Y - 1), ("t1c", t1, RING_Y), ("lh", lh, tasks - 1), ("ll", ll, tasks - 1),
+        ("ey", eh, RING_Y - 1), ("ec", eh, RING_Y), ("ely", el, RING_Y - 1), ("elc", el, RING_Y),
+        ("dl", dl, tasks - 1), ("dr", dr, tasks - 1), ("rl", wls, tiles - 1), ("al", wlg, tiles - 1),
+        ("rr", wrs, tiles - 1), ("ar", wrg, tiles - 1),
     ):
         wait(ref, count, send_sem, name)
-
-    @pl.when(jnp.logical_not(alone))
-    def _():
-        wait(la, 1, send_sem, "pm")
+    for a in range(RING_X):
+        wait(a2, RING_Z - (a == 0), send_sem, "a2" + str(a))
+        wait(c2, RING_Z - (a == 0), send_sem, "c2" + str(a))
 
 
 def on_device(deltas, sketches):
@@ -476,6 +461,7 @@
     gram_in = pltpu.VMEM((tiles, 2, LANES), F32)
     gram_own = pltpu.VMEM((2, LANES), F32)
     gram_all = pltpu.VMEM((tasks, 2, LANES), F32)
+    rows_all = pltpu.VMEM((tasks, tiles // tasks, RANK, LANES), BF16)
     piece = pltpu.VMEM((tiles, 8, LANES), F32)
     return pl.pallas_call(
         kernel,
@@ -486,8 +472,8 @@
             pltpu.VMEM((rows, width), BF16), pltpu.VMEM((RANK, width), BF16),
             half, half, half, gram_own, gram_in,
             half, half, half, half, half,
-            gram_own, gram_in, gram_own, gram_in, gram_all, gram_all,
-            pltpu.VMEM((RANK, LANES), F32), pltpu.VMEM((tasks, RANK, LANES), F32), pltpu.VMEM(block, F32),
+            half, gram_own, gram_in, gram_own, gram_in, gram_all, gram_all,
+            pltpu.VMEM((tasks, RANK, LANES), F32), rows_all, rows_all,
             pltpu.VMEM((tasks, RANK, width), BF16), pltpu.VMEM((tasks, RANK, width), BF16),
             piece, piece, piece, piece, piece, piece,
             pltpu.SemaphoreType.DMA((CHUNKS + 1,)),
@@ -495,7 +481,7 @@
             pltpu.SemaphoreType.DMA((len(SEMS),)),
         ],
         compiler_params=pltpu.CompilerParams(
-            collective_id=0, has_side_effects=True, vmem_limit_bytes=60 * 2**20
+            collective_id=0, has_side_effects=True, vmem_limit_bytes=52 * 2**20
         ),
     )(deltas, jnp.swapaxes(sketches, 1, 2))
 

time: 78.2 us -> 73.7 us (0.942)
  Pallas kernels: 76.3 us -> 72.1 us
    pallas_call x1, Pallas kernels: 76.3 us -> 72.1 us  [on_device(): pl.pallas_call(kernel, out_shape=jax.ShapeDtypeStruct((rows // tasks, wid...]
    unnamed x1 -> x3, local copies, waits for them, and re-layouts: 1.67 us -> 1.42 us
where the time goes in v3:
time: 73.7 us; the launch traced here: 73.5 us
  Pallas kernels  72.1 us (98%)
  local copies, waits for them, and re-layouts  1.42 us (2%)
    pallas_call x1, Pallas kernels, on_device(): pl.pallas_call(kernel, out_shape=jax.ShapeDtypeStruct((rows // tasks, wid...  72.1 us

profile of v3, /device:TPU:1, one launch (start us, length us, event | category | flops | bytes accessed | tf_op | source)
XLA Modules:
  0.0 73.5 jit_solution(17792043308384105500)
XLA Ops:
  0.0 0.0 copy-start
  0.0 0.7 copy-done
  0.7 72.1 %shard_map.28 = bf16[256,512]{1,0:T(8,128)(2,1)S(1)} custom-call(bf16[1,4096,512]{2,1,0:T(8,128)(2,1)} %d_hbm.1, bf16[1,16,512]{2,1,0:T(8,128)(2,1)S(1)} %bitcast.1), custom_call_target="tpu_custom_call" | custom-call | tf_op jit(solution)/shard_map/pallas_call | solution.py:466
  72.8 0.7 copy.4
Async XLA Ops:
  0.0 0.7 copy-start

commit v4 on v3

--- a/solution.py
+++ b/solution.py
@@ -366,11 +366,9 @@
     low = received("c1x", c1xs[me_j], c1xr)
     (left_slice,) = forward_solve(power_factor, [high + low])
     c2x[me_j] = (left_slice - c2[me_j].astype(F32)).astype(BF16)
-    gather("c2x", c2x)
     t1[me_t] = left_slice
     gls[...] = pack(dot_high(left_slice, left_slice, NT))
     to_task("t1", t1)
-    to_each("gl", gls, glr)
 
     right = project("c2", c2)
     high, low = split(right)
@@ -378,11 +376,11 @@
     to_task("e", eh)
     grs[...] = pack(dot_high(right, right, NT))
     to_each("gr", grs, grr)
+    gather("c2x", c2x)
+    to_each("gl", gls, glr)
     el[me_t] = low
     to_task("el", el)
 
-    dl[me_t] = received("gl", gls[...], glr)
-    to_task_direct("dl", lambda t: dl.at[me_t], dl)
     pass_on("t1", t1)
     wait(t1, RING_Y, recv_sem, "t1c")
     stacked = split(jnp.concatenate([t1[t] for t in range(tasks)], axis=0))
@@ -395,16 +393,20 @@
     store_pieces(wrs, fold(dot(stacked, stacked, NT)))
     scatter("rr", wrs, wrr)
 
-    wait(c2x, tiles - 1, recv_sem, "c2x")
-    for name, src, dst in (("lh", c2, lh), ("ll", c2x, ll)):
+    def left_rows(name, src, dst):
         to_task_direct(name, lambda t: src.at[pl.ds(t * per_task, per_task)], dst)
         dst[me_t] = src[pl.ds(me_t * per_task, per_task)]
 
+    left_rows("lh", c2, lh)
+    dl[me_t] = received("gl", gls[...], glr)
+    to_task_direct("dl", lambda t: dl.at[me_t], dl)
     dr[me_t] = received("gr", grs[...], grr)
     to_task_direct("dr", lambda t: dr.at[me_t], dr)
-    pass_on("el", el)
     wlg[me_j] = received("rl", wls[me_j], wlr)
     gather("al", wlg)
+    wait(c2x, tiles - 1, recv_sem, "c2x")
+    left_rows("ll", c2x, ll)
+    pass_on("el", el)
     wrg[me_j] = received("rr", wrs[me_j], wrr)
     gather("ar", wrg)
 
@@ -483,7 +485,10 @@
         compiler_params=pltpu.CompilerParams(
             collective_id=0, has_side_effects=True, vmem_limit_bytes=52 * 2**20
         ),
-    )(deltas, jnp.swapaxes(sketches, 1, 2))
+    )(
+        pltpu.with_memory_space_constraint(deltas, pltpu.HBM),
+        pltpu.with_memory_space_constraint(jnp.swapaxes(sketches, 1, 2), pltpu.HBM),
+    )
 
 
 def solution(mesh):

time: 73.7 us -> 70.2 us (0.953)
  Pallas kernels: 72.1 us -> 69.3 us
    pallas_call x1, Pallas kernels: 72.1 us -> 69.3 us  [on_device(): pl.pallas_call(kernel, out_shape=jax.ShapeDtypeStruct((rows // tasks, wid...]
where the time goes in v4:
time: 70.2 us; the launch traced here: 70 us
  Pallas kernels  69.3 us (99%)
  local copies, waits for them, and re-layouts  0.71 us (1%)
    pallas_call x1, Pallas kernels, on_device(): pl.pallas_call(kernel, out_shape=jax.ShapeDtypeStruct((rows // tasks, wid...  69.3 us

profile of v4, /device:TPU:1, one launch (start us, length us, event | category | flops | bytes accessed | tf_op | source)
XLA Modules:
  0.0 70.0 jit_solution(9300900411553310590)
XLA Ops:
  0.0 69.3 %shard_map.28 = bf16[256,512]{1,0:T(8,128)(2,1)S(1)} custom-call(bf16[1,4096,512]{2,1,0:T(8,128)(2,1)} %d_hbm.1, bf16[1,16,512]{2,1,0:T(8,128)(2,1)} %bitcast.1), custom_call_target="tpu_custom_call" | custom-call | tf_op jit(solution)/shard_map/pallas_call | solution.py:468
  69.3 0.7 %copy.4 = bf16[256,512]{1,0:T(8,128)(2,1)} copy(bf16[256,512]{1,0:T(8,128)(2,1)S(1)} %shard_map.28) | data formatting | bytes 524288

commit v5 on v4

--- a/solution.py
+++ b/solution.py
@@ -23,7 +23,7 @@
 TN = (((0,), (0,)), ((), ()))
 
 SEMS = ("a1", "a20", "a21", "a22", "a23", "gp", "c1", "c1x", "c20", "c21", "c22", "c23", "c2x", "gl", "t1y", "t1c",
-        "lh", "ll", "ey", "ec", "ely", "elc", "gr", "dl", "dr", "rl", "al", "rr", "ar")
+        "lh", "ll", "en", "ey", "ec", "ely", "elc", "gr", "dl", "dr", "rl", "al", "rr", "ar")
 SEM = {name: index for index, name in enumerate(SEMS)}
 
 
@@ -373,7 +373,9 @@
     right = project("c2", c2)
     high, low = split(right)
     eh[me_t] = high
-    to_task("e", eh)
+    for c in Y_STEPS:
+        send(eh.at[me_t], eh.at[me_t], "ey" if around(c, RING_Y) > 2 else "en", ys[c] + core, me_j)
+    send(eh.at[me_t], eh.at[me_t], "ec", twin, me_j)
     grs[...] = pack(dot_high(right, right, NT))
     to_each("gr", grs, grr)
     gather("c2x", c2x)
@@ -387,7 +389,11 @@
     store_pieces(wls, fold(dot_split(stacked, stacked, NT)))
     scatter("rl", wls, wlr)
 
-    pass_on("e", eh)
+    for name, near in (("en", True), ("ey", False)):
+        group = [c for c in Y_STEPS if (around(c, RING_Y) <= 2) == near]
+        wait(eh, len(group), recv_sem, name)
+        for c in group:
+            send(eh.at[ys[c] + core], eh.at[ys[c] + core], "ec", twin, me_j)
     wait(eh, RING_Y, recv_sem, "ec")
     stacked = jnp.concatenate([eh[t] for t in range(tasks)], axis=0)
     store_pieces(wrs, fold(dot(stacked, stacked, NT)))
@@ -397,13 +403,13 @@
         to_task_direct(name, lambda t: src.at[pl.ds(t * per_task, per_task)], dst)
         dst[me_t] = src[pl.ds(me_t * per_task, per_task)]
 
-    left_rows("lh", c2, lh)
     dl[me_t] = received("gl", gls[...], glr)
     to_task_direct("dl", lambda t: dl.at[me_t], dl)
     dr[me_t] = received("gr", grs[...], grr)
     to_task_direct("dr", lambda t: dr.at[me_t], dr)
     wlg[me_j] = received("rl", wls[me_j], wlr)
     gather("al", wlg)
+    left_rows("lh", c2, lh)
     wait(c2x, tiles - 1, recv_sem, "c2x")
     left_rows("ll", c2x, ll)
     pass_on("el", el)
@@ -445,7 +451,7 @@
         ("a1", a1s, tiles - 1), ("gp", gpr, tiles - 1), ("c1", c1s, tiles - 1), ("c1x", c1xs, tiles - 1),
         ("c2x", c2x, tiles - 1), ("gl", glr, tiles - 1), ("gr", grr, tiles - 1),
         ("t1y", t1, RING_Y - 1), ("t1c", t1, RING_Y), ("lh", lh, tasks - 1), ("ll", ll, tasks - 1),
-        ("ey", eh, RING_Y - 1), ("ec", eh, RING_Y), ("ely", el, RING_Y - 1), ("elc", el, RING_Y),
+        ("en", eh, 4), ("ey", eh, RING_Y - 5), ("ec", eh, RING_Y), ("ely", el, RING_Y - 1), ("elc", el, RING_Y),
         ("dl", dl, tasks - 1), ("dr", dr, tasks - 1), ("rl", wls, tiles - 1), ("al", wlg, tiles - 1),
         ("rr", wrs, tiles - 1), ("ar", wrg, tiles - 1),
     ):

time: 70.2 us -> 72.3 us (1.030)
  Pallas kernels: 69.3 us -> 71.5 us
    pallas_call x1, Pallas kernels: 69.3 us -> 71.5 us  [on_device(): pl.pallas_call(kernel, out_shape=jax.ShapeDtypeStruct((rows // tasks, wid...]
where the time goes in v5:
time: 72.3 us; the launch traced here: 72.2 us
  Pallas kernels  71.5 us (99%)
    pallas_call x1, Pallas kernels, on_device(): pl.pallas_call(kernel, out_shape=jax.ShapeDtypeStruct((rows // tasks, wid...  71.5 us

profile of v5, /device:TPU:1, one launch (start us, length us, event | category | flops | bytes accessed | tf_op | source)
XLA Modules:
  0.0 72.2 jit_solution(5834501753110646444)
XLA Ops:
  0.0 71.5 %shard_map.28 = bf16[256,512]{1,0:T(8,128)(2,1)S(1)} custom-call(bf16[1,4096,512]{2,1,0:T(8,128)(2,1)} %d_hbm.1, bf16[1,16,512]{2,1,0:T(8,128)(2,1)} %bitcast.1), custom_call_target="tpu_custom_call" | custom-call | tf_op jit(solution)/shard_map/pallas_call | solution.py:474
  71.5 0.7 copy.4
